TPU v7x, 128 devices: a whole 4x4x4 slice. The times are simulated.
128 devices in a mesh: row: 8 (over z_lo, x), col: 16 (over z_hi, y, core).
Axes of the slice: x: 4, y: 4, z: 4 (z_hi: 2, z_lo: 2; z = z_hi * 2 + z_lo), core: 2. Of those that a mesh axis runs over, the one named last changes fastest.
Arguments:
- trial: float32 [524288], P(('row', 'col')), may hold values from -6 to 6
- energies: float32 [524288], P(('row', 'col')), may hold values from 0.5 to 3
- densities: bfloat16 [8192, 64, 512], P(('row', 'col')), may hold values from -0.75 to 0.75
- screening: bfloat16 [1048576, 512], P(('row', 'col')), may hold values from 0.0099487305 to 0.099609375
- pair_index: int32 [2, 1048576], P(None, ('row', 'col')), may hold values from 0 to 8191, as said below
- pair_count: int32 [128], P(('row', 'col')), may hold values from 1024 to 8192, as said below
- recycled: float32 [20, 524288], P(None, ('row', 'col'))
Outputs:
- image: float32 [524288], P(('row', 'col'))
- coefficients: float32 [20], replicated
Inputs may be any that keep to these rules, and one draw needn't show every extreme that they name: `pair_index`: slot p of device d = p // 8192 (devices numbered row-major over row and col) holds rows[p] among the k-points of the devices in d's row index and cols[p] among those of the devices in d's col index. `pair_count`: one device is full in every draw.
All inputs are finite; a program needn't handle non-finite values.
Results may differ from a plain program's by a relative error of at most 0.014.
Values may be sent and summed in bfloat16 or wider, within the bound.
No kernel may reach another device: no remote copies, remote signals or barrier semaphores. Data moves between devices by JAX's collectives and lax.ppermute only.
A program may use at most 192 MiB of HBM per device.

v0:
```python
import math

import jax
import jax.numpy as jnp
from jax import lax
from jax.sharding import PartitionSpec as P


def add_terms(totals, table, source_index, target_index, weights):
    picked = jnp.take(table, source_index, axis=0).astype(jnp.float32)
    slot_terms = (weights * picked).astype(jnp.bfloat16)
    slot_terms = lax.optimization_barrier(slot_terms)
    return totals.at[target_index].add(slot_terms.astype(jnp.float32))


def pair_loop(live_count, capacity, handle, initial):
    block_rows = math.gcd(capacity, 1024)
    steps_needed = (live_count + block_rows - 1) // block_rows

    def advance(block_index, totals):
        return handle(block_index * block_rows, block_rows, totals)

    return lax.fori_loop(0, steps_needed, advance, initial)


def gather_row_block(values):
    return lax.all_gather(values, "col", axis=0, tiled=True)


def gather_col_block(values):
    return lax.all_gather(values, "row", axis=0, tiled=True)


def reduce_row_block(totals):
    return lax.psum_scatter(
        totals.astype(jnp.bfloat16), "col", scatter_dimension=0, tiled=True
    ).astype(jnp.float32)


def reduce_col_block(totals):
    return lax.psum_scatter(
        totals.astype(jnp.bfloat16), "row", scatter_dimension=0, tiled=True
    ).astype(jnp.float32)


def body(trial, energies, densities, screening, pair_index, pair_count, recycled):
    kpoints, transitions, gvectors = densities.shape
    row_devices = lax.axis_size("row")
    col_devices = lax.axis_size("col")
    row_place = lax.axis_index("row")
    capacity = screening.shape[0]
    live_count = pair_count[0]
    trial_b = trial.reshape(kpoints, transitions).astype(jnp.bfloat16)
    local_dens = jnp.einsum(
        "kt,ktg->kg", trial_b, densities, preferred_element_type=jnp.float32
    ).astype(jnp.bfloat16)

    def slot_data(first_slot, block_rows, row_source, col_source):
        weights = lax.dynamic_slice_in_dim(screening, first_slot, block_rows, 0).astype(jnp.float32)
        live_slots = first_slot + jnp.arange(block_rows) < live_count
        weights = jnp.where(live_slots[:, None], weights, 0.0)
        row_take = lax.dynamic_slice_in_dim(row_source, first_slot, block_rows, 0)
        col_take = lax.dynamic_slice_in_dim(col_source, first_slot, block_rows, 0)
        return (weights, row_take, col_take)

    row_local = pair_index[0] - row_place * col_devices * kpoints
    col_local = pair_index[1] // (col_devices * kpoints) * kpoints + pair_index[1] % kpoints
    row_zeros = jnp.zeros((col_devices * kpoints, gvectors), jnp.float32)
    col_zeros = jnp.zeros((row_devices * kpoints, gvectors), jnp.float32)
    row_dens = gather_row_block(local_dens)
    col_dens = gather_col_block(local_dens)

    def handle_both(first_slot, block_rows, totals):
        weights, row_take, col_take = slot_data(first_slot, block_rows, row_local, col_local)
        row_totals = add_terms(totals[0], col_dens, col_take, row_take, weights)
        col_totals = add_terms(totals[1], row_dens, row_take, col_take, weights)
        return (row_totals, col_totals)

    row_totals, col_totals = pair_loop(live_count, capacity, handle_both, (row_zeros, col_zeros))
    field_sum = reduce_row_block(row_totals) + reduce_col_block(col_totals)
    field_b = field_sum.astype(jnp.bfloat16)
    kernel_part = jnp.einsum("kg,ktg->kt", field_b, densities, preferred_element_type=jnp.float32)
    product = energies * trial + kernel_part.reshape(kpoints * transitions)
    local_proj = jnp.dot(recycled, product, precision=lax.Precision.HIGHEST)
    coefficients = lax.psum(local_proj, ("row", "col"))
    image = product - jnp.dot(coefficients, recycled, precision=lax.Precision.HIGHEST)
    return (image, coefficients)


def solution(mesh):
    placed = (
        P(("row", "col")),
        P(("row", "col")),
        P(("row", "col"), None, None),
        P(("row", "col"), None),
        P(None, ("row", "col")),
        P(("row", "col")),
        P(None, ("row", "col")),
    )
    return jax.shard_map(
        body, mesh=mesh, in_specs=placed, out_specs=(P(("row", "col")), P()), check_vma=False
    )
```

profile of v0, /device:TPU:1, one launch (start us, length us, event | category | flops | bytes accessed | tf_op | source)
XLA Modules:
  0.0 509.5 jit_solution(15924236205525941503)
XLA Ops:
  7.2 0.0 copy-start
  7.2 0.0 all-gather.2.cloned.1.call-start
  7.2 0.8 convert_element_type.45
  8.0 0.1 reshape.72
  8.1 2.9 fusion.15
  10.9 0.6 copy.16
  11.6 0.0 all-gather.2.cloned.1.call-update
  11.6 0.0 reduce-scatter.5.cloned.1.call-start
  12.3 0.0 copy-done.3
  12.4 24.8 %all_gather.6 = bf16[512,512]{1,0:T(8,128)(2,1)S(1)} all-gather(bf16[64,512]{1,0:T(8,128)(2,1)} %bitcast.25), channel_id=1, replica_groups=mesh['row'=8,'col'=16] {'row'}, dimensions={0}, use_global_device_ids=true | all-gather | bytes 589824 | tf_op jit(solution)/shard_map/all_gather | solution.py:31
  37.2 23.4 %all-gather.2.cloned.1.call-done = bf16[1024,512]{1,0:T(8,128)(2,1)} async-done(((bf16[64,512]{1,0:T(8,128)(2,1)}), bf16[1024,512]{1,0:T(8,128)(2,1)}) %all-gather.2.cloned.1.call-update) | async-done | bytes 1048592 | tf_op jit(solution)/shard_map/all_gather | solution.py:27
  60.6 1.1 broadcast_in_dim.44
  61.7 1.6 broadcast_in_dim.43
  63.3 0.0 copy-done.1
  63.3 65.8 %while.12 = (s32[]{:T(128)}, f32[1024,512]{1,0:T(8,128)}, f32[512,512]{1,0:T(8,128)}, s32[]{:T(128)}, s32[8192]{0:T(1024)S(1)}, /*index=5*/s32[]{:T(128)}, bf16[...) while((s32[]{:T(128)}, f32[1024,512]{1,0:T(8,128)}, ...), condition=%wide.region_3.4_spmd, body=%wide.region_0.3_spmd.sunk | while | flops 7356422 | bytes 14727367 | solution.py:23
  63.3 0.7 compare_and_fusion.4
  64.0 5.1 %gather_fusion = bf16[1024,512]{1,0:T(8,128)(2,1)} fusion(bf16[1024,512]{1,0:T(8,128)(2,1)S(1)} %get-tuple-element.200, s32[1024]{0:T(1024)S(1)} %broadcast_clamp_fusion.4), kind=kCustom, calls=%fused_computation.1.clone.1 | custom fusion | bytes 2101248 | tf_op jit(solution)/shard_map/while/body/jit(_take)/gather | solution.py:10
  69.1 5.0 gather_fusion.1
  74.2 3.1 multiply_convert_fusion.3
  77.3 9.4 %scatter_custom_fusion.11 = f32[512,512]{1,0:T(8,128)} fusion(f32[512,512]{1,0:T(8,128)} %get-tuple-element.179, s32[1024]{0:T(1024)S(1)} %get-tuple-element.159, bf16[1024,512]{1,0:T(8,128)(2,1)} %get-tuple-element.162), kind=kCustom, calls=%fused_computation.4.clone.1 | custom fusion | flops 1048576 | bytes 2097152 | tf_op jit(solution)/shard_map/while/body/scatter-add | solution.py:13
  86.6 9.6 %scatter_custom_fusion.10 = f32[1024,512]{1,0:T(8,128)} fusion(f32[1024,512]{1,0:T(8,128)} %get-tuple-element.178, s32[1024]{0:T(1024)S(1)} %get-tuple-element.156, bf16[1024,512]{1,0:T(8,128)(2,1)S(1)} %get-tuple-element.161), kind=kCustom, calls=%fused_computation.7.clone.1 | custom fusion | flops 1048576 | bytes 3145728 | tf_op jit(solution)/shard_map/while/body/scatter-add | solution.py:13
  96.3 0.7 compare_and_fusion.4
  96.9 5.1 %gather_fusion = bf16[1024,512]{1,0:T(8,128)(2,1)} fusion(bf16[1024,512]{1,0:T(8,128)(2,1)S(1)} %get-tuple-element.200, s32[1024]{0:T(1024)S(1)} %broadcast_clamp_fusion.4), kind=kCustom, calls=%fused_computation.1.clone.1 | custom fusion | bytes 2101248 | tf_op jit(solution)/shard_map/while/body/jit(_take)/gather | solution.py:10
  102.0 5.0 gather_fusion.1
  107.1 3.1 multiply_convert_fusion.3
  110.2 9.4 %scatter_custom_fusion.11 = f32[512,512]{1,0:T(8,128)} fusion(f32[512,512]{1,0:T(8,128)} %get-tuple-element.179, s32[1024]{0:T(1024)S(1)} %get-tuple-element.159, bf16[1024,512]{1,0:T(8,128)(2,1)} %get-tuple-element.162), kind=kCustom, calls=%fused_computation.4.clone.1 | custom fusion | flops 1048576 | bytes 2097152 | tf_op jit(solution)/shard_map/while/body/scatter-add | solution.py:13
  119.6 9.6 %scatter_custom_fusion.10 = f32[1024,512]{1,0:T(8,128)} fusion(f32[1024,512]{1,0:T(8,128)} %get-tuple-element.178, s32[1024]{0:T(1024)S(1)} %get-tuple-element.156, bf16[1024,512]{1,0:T(8,128)(2,1)S(1)} %get-tuple-element.161), kind=kCustom, calls=%fused_computation.7.clone.1 | custom fusion | flops 1048576 | bytes 3145728 | tf_op jit(solution)/shard_map/while/body/scatter-add | solution.py:13
  129.2 2.2 convert_element_type.50
  131.4 0.0 reduce-scatter.5.cloned.1.call-update
  131.4 0.0 reduce-scatter.3.cloned.1.call-start
  131.5 0.0 copy-done.2
  131.5 1.1 convert_element_type.48
  132.6 0.0 reduce-scatter.3.cloned.1.call-update
  132.6 225.3 %reduce-scatter.5.cloned.1.call-done = bf16[64,512]{1,0:T(8,128)(2,1)} async-done(((bf16[512,512]{1,0:T(8,128)(2,1)}), bf16[64,512]{1,0:T(8,128)(2,1)}) %reduce-scatter.5.cloned.1.call-update) | async-done | bytes 65552 | tf_op jit(solution)/shard_map/reduce_scatter | solution.py:41
  357.9 73.1 %reduce-scatter.3.cloned.1.call-done = bf16[64,512]{1,0:T(8,128)(2,1)} async-done(((bf16[1024,512]{1,0:T(8,128)(2,1)}), bf16[64,512]{1,0:T(8,128)(2,1)}) %reduce-scatter.3.cloned.1.call-update) | async-done | bytes 65552 | tf_op jit(solution)/shard_map/reduce_scatter | solution.py:35
  431.0 0.9 fusion.6
  431.9 0.0 copy-start.4
  431.9 0.0 copy-start.5
  431.9 3.4 fusion.4
  435.3 0.1 reshape.26
  435.4 0.0 copy-done.4
  435.4 0.0 copy-done.5
  435.4 0.0 copy-done
  435.4 0.5 convolution_bitcast_fusion
  435.9 66.1 %psum.7 = f32[20]{0:T(128)S(1)} all-reduce(f32[20]{0:T(128)S(1)} %convolution_bitcast_fusion), channel_id=1, replica_groups=mesh['row'=8,'col'=16] {'row','col'}, use_global_device_ids=true, to_apply=%region_6.7 | all-reduce | flops 20 | bytes 160 | tf_op jit(solution)/shard_map/psum | solution.py:85
  502.0 0.3 fusion.12
  502.3 0.6 sub.31
  502.9 0.0 copy-done.6
  (13 shorter events, 0.1 us)
Async XLA Ops:
  7.2 428.3 %copy-start = (f32[20,4096]{1,0:T(8,128)S(1)}, f32[20,4096]{1,0:T(8,128)}, u32[]{:S(2)}) copy-start(f32[20,4096]{1,0:T(8,128)} %param.15) | copy-start | bytes 983044
  7.2 53.4 %all-gather.2.cloned.1.call-start = ((), (), s32[]{:S(2)}) async-start(), calls=%async_computation.2 | async-start | bytes 1114112 | tf_op jit(solution)/shard_map/all_gather | solution.py:27
  8.1 4.3 copy-start.3
  11.6 346.3 %reduce-scatter.5.cloned.1.call-start = ((), (), s32[]{:S(2)}) async-start(), calls=%async_computation.4 | async-start | bytes 589824 | tf_op jit(solution)/shard_map/reduce_scatter | solution.py:41
  60.6 2.8 copy-start.1
  129.2 2.3 copy-start.2
  131.4 299.6 %reduce-scatter.3.cloned.1.call-start = ((), (), s32[]{:S(2)}) async-start(), calls=%async_computation.3 | async-start | bytes 1114112 | tf_op jit(solution)/shard_map/reduce_scatter | solution.py:35
  431.9 3.5 copy-start.4
  431.9 3.5 copy-start.5
  502.0 0.9 copy-start.6
Sparse Core Ops, SparseCore 0:
  11.7 48.7 all-gather.1
  131.5 226.3 reduce-scatter.4
  362.2 68.7 reduce-scatter.2
where the time goes:
time: 511 us; the launch traced here: 509 us
  waiting for transfers between devices  322 us (63%)
  blocking collectives  90.8 us (18%)
  other arithmetic  51.2 us (10%)
  local copies, waits for them, and re-layouts  23.9 us (5%)
  between operations  14.5 us (3%)
  matrix products  7.02 us (1%)
    reduce_scatter x1, waiting for transfers between devices, reduce_col_block(): lax.psum_scatter(totals.astype(jnp.bfloat16), 'row', scatter_dimension=0,...  225 us
    reduce_scatter x1, waiting for transfers between devices, reduce_row_block(): lax.psum_scatter(totals.astype(jnp.bfloat16), 'col', scatter_dimension=0,...  73.1 us
    psum x1, blocking collectives, body(): coefficients = lax.psum(local_proj, ('row', 'col'))  66.1 us
    scatter-add x4, other arithmetic, add_terms(): return totals.at[target_index].add(slot_terms.astype(jnp.float32))  38 us
    all_gather x1, blocking collectives, gather_col_block(): return lax.all_gather(values, 'row', axis=0, tiled=True)  24.8 us
    all_gather x1, waiting for transfers between devices, gather_row_block(): return lax.all_gather(values, 'col', axis=0, tiled=True)  23.4 us
    gather x4, local copies, waits for them, and re-layouts, add_terms(): picked = jnp.take(table, source_index, axis=0).astype(jnp.float32)  20.3 us
  transfers between devices with their start and end apart: 3, of which 3 were waited for; matrix products, arithmetic and copies ran while one was open for 0% of the time, Pallas kernels for 0%

commit v1 on v0

v1 whole, which is shorter than its diff:
```python
import functools

import jax
import jax.numpy as jnp
from jax import lax
from jax.experimental import pallas as pl
from jax.experimental.pallas import tpu as pltpu
from jax.sharding import Mesh, PartitionSpec as P

AXES = ("zl", "x", "zh", "y", "c")
F32 = jnp.float32
BF16 = jnp.bfloat16
CHUNK = 512
COPIES = 4
UNROLL = 4


def slot_kernel(rows, cols, count, weights, own_dens, other_dens, col_dens,
                own_total, other_total, col_total, weight_buf, spread, *rest):
    row_tables, col_tables, sem = rest[:COPIES], rest[COPIES:2 * COPIES], rest[2 * COPIES]
    live = count[0]
    chunks = (live + CHUNK - 1) // CHUNK

    def copy(i):
        part = pl.ds(i * CHUNK, CHUNK)
        return pltpu.make_async_copy(weights.at[part], weight_buf.at[part], sem.at[i])

    def start(i, _):
        copy(i).start()
        return 0

    lax.fori_loop(0, chunks, start, 0)
    zeros = jnp.zeros((4, 128), F32)

    def fill(source, tables, first, dens_first):
        def step(i, _):
            part = source[pl.ds(pl.multiple_of(i * 16, 16), 16), :].astype(F32)
            for t in range(4):
                dens = part[4 * t:4 * t + 4]
                entry = jnp.concatenate([dens, zeros] if dens_first else [zeros, dens], 0)
                for table in tables:
                    table[pl.ds(pl.multiple_of((first + i * 4 + t) * 8, 8), 8), :] = entry
            return 0

        lax.fori_loop(0, source.shape[0] // 16, step, 0, unroll=2)

    half = own_dens.shape[0] // 4
    fill(own_dens, row_tables, 0, True)
    fill(other_dens, row_tables, half, True)
    fill(col_dens, col_tables, 0, False)

    def one(slot, group, lane, which):
        low = lax.broadcasted_iota(jnp.int32, (8, 128), 0) >= 4
        w = spread[pl.ds(group * 64 + lane, 8, stride=8), :]
        r = pl.ds(pl.multiple_of(rows[slot], 8), 8)
        c = pl.ds(pl.multiple_of(cols[slot], 8), 8)
        row_entry = row_tables[which][r, :]
        col_entry = col_tables[which][c, :]
        row_tables[which][r, :] = row_entry + jnp.where(low, w, 0.0) * col_entry
        col_tables[which][c, :] = col_entry + jnp.where(low, 0.0, w) * row_entry

    def chunk(i, _):
        copy(i).wait()
        left = jnp.minimum(live - i * CHUNK, CHUNK)

        def relayout(g, _):
            v = weight_buf[pl.ds(pl.multiple_of(i * CHUNK + g * 16, 16), 16), :].astype(F32)
            for h in range(2):
                for j in range(4):
                    tile = v[8 * h:8 * h + 8, 128 * j:128 * j + 128]
                    for twice in range(2):
                        at = g * 128 + h * 64 + twice * 32 + j * 8
                        spread[pl.ds(pl.multiple_of(at, 8), 8), :] = tile
            return 0

        lax.fori_loop(0, CHUNK // 16, relayout, 0, unroll=2)
        wide = left // (8 * UNROLL)

        def groups(g, _):
            for t in range(UNROLL):
                for u in range(8):
                    group = g * UNROLL + t
                    one(i * CHUNK + group * 8 + u, group, u, u % COPIES)
            return 0

        lax.fori_loop(0, wide, groups, 0)

        def tail(t, _):
            slot = wide * 8 * UNROLL + t
            one(i * CHUNK + slot, slot // 8, slot % 8, 0)
            return 0

        lax.fori_loop(0, left - wide * 8 * UNROLL, tail, 0)
        return 0

    lax.fori_loop(0, chunks, chunk, 0)

    def drain(tables, first, target, at):
        def step(i, _):
            parts = []
            for t in range(4):
                entry = pl.ds(pl.multiple_of((first + i * 4 + t) * 8, 8), 8)
                total = tables[0][entry, :]
                for table in tables[1:]:
                    total = total + table[entry, :]
                parts.append(total[at:at + 4])
            rows16 = pl.ds(pl.multiple_of(i * 16, 16), 16)
            target[rows16, :] = jnp.concatenate(parts, 0).astype(BF16)
            return 0

        lax.fori_loop(0, target.shape[0] // 16, step, 0, unroll=4)

    drain(row_tables, 0, own_total, 4)
    drain(row_tables, half, other_total, 4)
    drain(col_tables, 0, col_total, 0)


def pair_terms(rows, cols, count, weights, own_dens, other_dens, col_dens):
    smem = pl.BlockSpec(memory_space=pltpu.SMEM)
    vmem = pl.BlockSpec(memory_space=pltpu.VMEM)
    outs = [jax.ShapeDtypeStruct(a.shape, BF16) for a in (own_dens, other_dens, col_dens)]
    row_table = pltpu.VMEM((4 * own_dens.shape[0], 128), F32)
    col_table = pltpu.VMEM((2 * col_dens.shape[0], 128), F32)
    return pl.pallas_call(
        slot_kernel,
        out_shape=outs,
        in_specs=[smem, smem, smem, pl.BlockSpec(memory_space=pl.ANY), vmem, vmem, vmem],
        out_specs=[vmem, vmem, vmem],
        scratch_shapes=[
            pltpu.VMEM(weights.shape, BF16),
            pltpu.VMEM((CHUNK * 8, 128), F32),
            *[row_table] * COPIES,
            *[col_table] * COPIES,
            pltpu.SemaphoreType.DMA((weights.shape[0] // CHUNK,)),
        ],
        compiler_params=pltpu.CompilerParams(vmem_limit_bytes=56 * 2**20),
    )(rows, cols, count, weights, own_dens, other_dens, col_dens)


def body(trial, energies, densities, screening, pair_index, pair_count, recycled):
    kpoints, transitions, gvectors = densities.shape
    lanes = 128
    per_k = gvectors // lanes
    col_devices = lax.axis_size("zh") * lax.axis_size("y") * lax.axis_size("c")
    chips = lax.axis_size("zh") * lax.axis_size("y")
    row_place = lax.axis_index("zl") * lax.axis_size("x") + lax.axis_index("x")
    core = lax.axis_index("c")
    swap = [(0, 1), (1, 0)]

    row_local = pair_index[0] - row_place * col_devices * kpoints
    owner = row_local // kpoints
    rows = (((owner % 2) ^ core) * chips + owner // 2) * kpoints + row_local % kpoints
    cols = pair_index[1] // (col_devices * kpoints) * kpoints + pair_index[1] % kpoints

    trial_b = trial.reshape(kpoints, transitions).astype(BF16)
    local_dens = jnp.einsum(
        "kt,ktg->kg", trial_b, densities, preferred_element_type=F32
    ).astype(BF16).reshape(kpoints * per_k, lanes)

    def gather(values, axes):
        size = 1
        for a in axes:
            size *= lax.axis_size(a)
        spread = jnp.broadcast_to(values[None], (size,) + values.shape)
        return lax.all_to_all(spread, axes, 0, 0).reshape(-1, lanes)

    own_dens = gather(local_dens, ("zh", "y"))
    other_dens = lax.ppermute(own_dens, "c", swap)
    col_dens = gather(local_dens, ("zl", "x"))

    own_total, other_total, col_total = pair_terms(
        rows * 8, cols * 8, pair_count, screening, own_dens, other_dens, col_dens)

    def scatter(values, axes):
        parts = values.reshape(-1, kpoints * per_k, lanes)
        return jnp.sum(lax.all_to_all(parts, axes, 0, 0).astype(F32), 0)

    from_other = lax.ppermute(other_total, "c", swap)
    row_total = (own_total.astype(F32) + from_other.astype(F32)).astype(BF16)
    field = scatter(col_total, ("zl", "x")) + scatter(row_total, ("zh", "y"))
    field_b = field.astype(BF16).reshape(kpoints, gvectors)
    kernel_part = jnp.einsum("kg,ktg->kt", field_b, densities, preferred_element_type=F32)
    product = energies * trial + kernel_part.reshape(kpoints * transitions)
    local_proj = jnp.dot(recycled, product, precision=lax.Precision.HIGHEST)
    devices = col_devices * lax.axis_size("zl") * lax.axis_size("x")
    spread = jnp.broadcast_to(local_proj[None], (devices,) + local_proj.shape)
    coefficients = jnp.sum(lax.all_to_all(spread, AXES, 0, 0, tiled=True), 0)
    image = product - jnp.dot(coefficients, recycled, precision=lax.Precision.HIGHEST)
    return (image, coefficients)


def solution(mesh):
    fine = Mesh(mesh.devices.reshape(2, 4, 2, 4, 2), AXES)
    placed = (
        P(AXES),
        P(AXES),
        P(AXES, None, None),
        P(AXES, None),
        P(None, AXES),
        P(AXES),
        P(None, AXES),
    )
    return jax.shard_map(
        body, mesh=fine, in_specs=placed, out_specs=(P(AXES), P()), check_vma=False
    )
```

time: 511 us -> 115 us (0.23)
  waiting for transfers between devices: 322 us -> 39.2 us
  blocking collectives: 90.8 us -> 13.1 us
  other arithmetic: 51.2 us -> 4.49 us
  starting transfers between devices: 0.12 us -> 32.2 us
  local copies, waits for them, and re-layouts: 23.9 us -> 2.18 us
  Pallas kernels: 0 us -> 15.4 us
  between operations: 14.5 us -> 1.42 us
    reduce_scatter x2 -> x0, waiting for transfers between devices: 298 us -> none  [the longest x1 225 us: reduce_col_block(): lax.psum_scatter(totals.astype(jnp.bfloat16), 'row', scatter_dimension=0,...]
    psum x1 -> x0, blocking collectives: 66.1 us -> none  [body(): coefficients = lax.psum(local_proj, ('row', 'col'))]
    all_to_all x0 -> x4, waiting for transfers between devices: none -> 39.2 us  [the longest x2 19.8 us: scatter(): return jnp.sum(lax.all_to_all(parts, axes, 0, 0).astype(F32), 0)]
    scatter-add x4 -> x0, other arithmetic: 38 us -> none  [add_terms(): return totals.at[target_index].add(slot_terms.astype(jnp.float32))]
    all_to_all x0 -> x4, starting transfers between devices: none -> 31 us  [the longest x2 18.2 us: scatter(): return jnp.sum(lax.all_to_all(parts, axes, 0, 0).astype(F32), 0)]
    all_gather x1 -> x0, blocking collectives: 24.8 us -> none  [gather_col_block(): return lax.all_gather(values, 'row', axis=0, tiled=True)]
    all_gather x1 -> x0, waiting for transfers between devices: 23.4 us -> none  [gather_row_block(): return lax.all_gather(values, 'col', axis=0, tiled=True)]
    gather x4 -> x0, local copies, waits for them, and re-layouts: 20.3 us -> none  [add_terms(): picked = jnp.take(table, source_index, axis=0).astype(jnp.float32)]
  transfers between devices with their start and end apart: 3 -> 6, of which waited for: 3 -> 4; matrix products, arithmetic and copies ran while one was open for 0% -> 2% of each run, Pallas kernels for 0% -> 0%
where the time goes in v1:
time: 115 us
  waiting for transfers between devices  39.2 us (34%)
  starting transfers between devices  32.2 us (28%)
  Pallas kernels  15.4 us (13%)
  blocking collectives  13.1 us (11%)
  matrix products  6.98 us (6%)
  other arithmetic  4.49 us (4%)
  local copies, waits for them, and re-layouts  2.18 us (2%)
  between operations  1.42 us (1%)
    all_to_all x2, waiting for transfers between devices, scatter(): return jnp.sum(lax.all_to_all(parts, axes, 0, 0).astype(F32), 0)  19.8 us
    all_to_all x2, waiting for transfers between devices, gather(): return lax.all_to_all(spread, axes, 0, 0).reshape(-1, lanes)  19.3 us
    all_to_all x2, starting transfers between devices, scatter(): return jnp.sum(lax.all_to_all(parts, axes, 0, 0).astype(F32), 0)  18.2 us
    pallas_call x1, Pallas kernels, pair_terms(): pl.pallas_call(slot_kernel, out_shape=outs, in_specs=[smem, smem, smem, p...  15.4 us
    all_to_all x1, blocking collectives, body(): coefficients = jnp.sum(lax.all_to_all(spread, AXES, 0, 0, tiled=True), 0)  13.1 us
    all_to_all x2, starting transfers between devices, gather(): return lax.all_to_all(spread, axes, 0, 0).reshape(-1, lanes)  12.8 us
    dot_general x1, matrix products, body(): jnp.einsum('kg,ktg->kt', field_b, densities, preferred_element_type=F32)  3.36 us
    dot_general x1, matrix products, body(): jnp.einsum('kt,ktg->kg', trial_b, densities, preferred_element_type=F32)  2.84 us
  transfers between devices with their start and end apart: 6, of which 4 were waited for; matrix products, arithmetic and copies ran while one was open for 2% of the time, Pallas kernels for 0%

profile of v1, /device:TPU:1, one launch (start us, length us, event | category | flops | bytes accessed | tf_op | source)
XLA Modules:
  0.0 115.0 jit_solution(11906339961592787898)
XLA Ops:
  0.6 0.0 copy-start
  0.6 0.0 copy-start.4
  0.7 0.8 convert_element_type.31
  1.4 0.1 reshape.49
  1.5 2.8 %fusion.21 = bf16[64,1,512]{2,1,0:T(2,128)(2,1)S(1)} fusion(bf16[64,64,1]{1,2,0:T(2,128)(2,1)S(1)} %reshape.49, bf16[64,64,512]{2,1,0:T(8,128)(2,1)} %param.9), kind=kOutput, calls=%fused_computation.48 | convolution fusion | flops 4194304 | bytes 4268032 | tf_op jit(solution)/shard_map/kt,ktg->kg/dot_general | solution.py:156
  4.4 0.1 broadcast_in_dim.6
  4.4 0.9 broadcast_in_dim.7
  5.3 8.3 %all-to-all-start = ((bf16[8,256,128]{2,1,0:T(8,128)(2,1)}), bf16[8,256,128]{2,1,0:T(8,128)(2,1)S(1)}, u32[]{:S(2)}, u32[]{:S(2)}) async-start(bf16[8,256,128]{2,1,0:T(8,128)(2,1)} %broadcast_in_dim.7), calls=%async_computation | async-start | bytes 1048576 | tf_op jit(solution)/shard_map/all_to_all | solution.py:165
  13.6 11.7 %all-to-all-done = bf16[8,256,128]{2,1,0:T(8,128)(2,1)S(1)} async-done(((bf16[8,256,128]{2,1,0:T(8,128)(2,1)}), bf16[8,256,128]{2,1,0:T(8,128)(2,1)S(1)}, u32[]{:S(2)}, u32[]{:S(2)}) %all-to-all-start) | async-done | bytes 524320 | tf_op jit(solution)/shard_map/all_to_all | solution.py:165
  25.3 0.0 copy-start.1
  25.3 4.5 %all-to-all-start.1 = ((bf16[8,256,128]{2,1,0:T(8,128)(2,1)}), bf16[8,256,128]{2,1,0:T(8,128)(2,1)S(1)}, u32[]{:S(2)}, u32[]{:S(2)}) async-start(bf16[8,256,128]{2,1,0:T(8,128)(2,1)} %broadcast_in_dim.7), calls=%async_computation.1 | async-start | bytes 1048576 | tf_op jit(solution)/shard_map/all_to_all | solution.py:165
  29.8 1.1 collective-permute-start
  31.0 0.0 copy-done.4
  31.7 0.7 fusion.5
  32.4 7.6 %all-to-all-done.1 = bf16[8,256,128]{2,1,0:T(8,128)(2,1)S(1)} async-done(((bf16[8,256,128]{2,1,0:T(8,128)(2,1)}), bf16[8,256,128]{2,1,0:T(8,128)(2,1)S(1)}, u32[]{:S(2)}, u32[]{:S(2)}) %all-to-all-start.1) | async-done | bytes 524320 | tf_op jit(solution)/shard_map/all_to_all | solution.py:165
  40.0 0.0 copy-start.2
  40.0 0.0 collective-permute-done.other_dens
  40.0 0.0 copy-start.3
  40.0 0.0 copy-done.1
  40.0 0.8 copy-done.2
  40.8 0.2 copy-done.3
  41.0 15.4 %shard_map.86 = (bf16[2048,128]{1,0:T(8,128)(2,1)}, bf16[2048,128]{1,0:T(8,128)(2,1)}, bf16[2048,128]{1,0:T(8,128)(2,1)}) custom-call(s32[8192]{0:T(1024)} %get-tuple-element.10.rows, s32[8192]{0:T(1024)} %get-tuple-element.11.cols, s32[1]{0:T(128)S(6)} %copy.18.count, bf16[8192,512]{1,0:T(8,128)(2,1)} %weights.1, bf16[2048,128]{1,0:T(8,128)(2,1)} %bitcast.26, ...), custom_call_target="tpu_custom_call" | custom-call | tf_op jit(solution)/shard_map/pallas_call | solution.py:124
  56.4 0.1 collective-permute-start.1
  56.5 14.7 %all-to-all-start.2 = ((bf16[8,256,128]{2,1,0:T(8,128)(2,1)}), bf16[8,256,128]{2,1,0:T(8,128)(2,1)S(1)}, u32[]{:S(2)}, u32[]{:S(2)}) async-start(bf16[8,256,128]{2,1,0:T(8,128)(2,1)} %bitcast.28), calls=%async_computation.2 | async-start | bytes 1048576 | tf_op jit(solution)/shard_map/all_to_all | solution.py:176
  71.2 0.0 collective-permute-done.1
  71.2 0.0 copy-start.5
  71.2 0.0 copy-start.6
  71.2 2.0 %add_convert_fusion = bf16[2048,128]{1,0:T(8,128)(2,1)} fusion(bf16[2048,128]{1,0:T(8,128)(2,1)S(1)} %collective-permute-done.1, bf16[2048,128]{1,0:T(8,128)(2,1)} %get-tuple-element.6), kind=kLoop, calls=%fused_computation.2 | loop fusion | flops 1048576 | bytes 1572864 | tf_op jit(solution)/shard_map/convert_element_type | solution.py:179
  73.2 8.3 %all-to-all-done.2 = bf16[8,256,128]{2,1,0:T(8,128)(2,1)S(1)} async-done(((bf16[8,256,128]{2,1,0:T(8,128)(2,1)}), bf16[8,256,128]{2,1,0:T(8,128)(2,1)S(1)}, u32[]{:S(2)}, u32[]{:S(2)}) %all-to-all-start.2) | async-done | bytes 524320 | tf_op jit(solution)/shard_map/all_to_all | solution.py:176
  81.5 3.5 %all-to-all-start.3 = ((bf16[8,256,128]{2,1,0:T(8,128)(2,1)}), bf16[8,256,128]{2,1,0:T(8,128)(2,1)S(1)}, u32[]{:S(2)}, u32[]{:S(2)}) async-start(bf16[8,256,128]{2,1,0:T(8,128)(2,1)} %bitcast.6), calls=%async_computation.3 | async-start | bytes 1048576 | tf_op jit(solution)/shard_map/all_to_all | solution.py:176
  85.0 0.1 convert_reduce_fusion.1
  85.1 11.6 %all-to-all-done.3 = bf16[8,256,128]{2,1,0:T(8,128)(2,1)S(1)} async-done(((bf16[8,256,128]{2,1,0:T(8,128)(2,1)}), bf16[8,256,128]{2,1,0:T(8,128)(2,1)S(1)}, u32[]{:S(2)}, u32[]{:S(2)}) %all-to-all-start.3) | async-done | bytes 524320 | tf_op jit(solution)/shard_map/all_to_all | solution.py:176
  96.6 0.1 convert_reduce_fusion
  96.8 3.4 %fusion.22 = f32[64,1,64]{2,1,0:T(1,128)S(1)} fusion(bf16[64,512,1]{1,2,0:T(2,128)(2,1)S(1)} %reshape.51, bf16[64,64,512]{2,1,0:T(8,128)(2,1)} %param.9), kind=kOutput, calls=%fused_computation.49 | convolution fusion | flops 4194304 | bytes 4276224 | tf_op jit(solution)/shard_map/kg,ktg->kt/dot_general | solution.py:182
  100.1 0.1 reshape.39
  100.2 0.0 copy-done.5
  100.2 0.0 copy-done.6
  100.2 0.0 copy-done
  100.3 0.5 convolution_bitcast_fusion
  100.7 0.1 broadcast_in_dim.8
  100.8 13.1 %all_to_all.26 = f32[128,1,20]{2,1,0:T(1,128)S(1)} all-to-all(f32[128,1,20]{2,1,0:T(1,128)S(1)} %broadcast_in_dim.8), channel_id=1, replica_groups=mesh['zl'=2,'x'=4,'zh'=2,'y'=4,'c'=2] {'zl','x','zh','y','c'}, dimensions={0} | all-to-all | bytes 20480 | tf_op jit(solution)/shard_map/all_to_all | solution.py:187
  113.9 0.2 reduce_sum.29
  114.1 0.0 copy-start.7
  114.1 0.3 fusion.18
  114.4 0.6 sub.32
  115.0 0.0 copy-done.7
  (5 shorter events, 0.1 us)
Async XLA Ops:
  0.6 99.6 %copy-start = (f32[20,4096]{1,0:T(8,128)S(1)}, f32[20,4096]{1,0:T(8,128)}, u32[]{:S(2)}) copy-start(f32[20,4096]{1,0:T(8,128)} %param.13) | copy-start | bytes 983044
  0.6 30.3 %copy-start.4 = (s32[2,8192]{1,0:T(2,128)S(1)}, s32[2,8192]{1,0:T(2,128)}, u32[]{:S(2)}) copy-start(s32[2,8192]{1,0:T(2,128)} %param.11) | copy-start | bytes 196612
  5.3 20.0 %all-to-all-start = ((bf16[8,256,128]{2,1,0:T(8,128)(2,1)}), bf16[8,256,128]{2,1,0:T(8,128)(2,1)S(1)}, u32[]{:S(2)}, u32[]{:S(2)}) async-start(bf16[8,256,128]{2,1,0:T(8,128)(2,1)} %broadcast_in_dim.7), calls=%async_computation | async-start | bytes 1048576 | tf_op jit(solution)/shard_map/all_to_all | solution.py:165
  25.3 14.7 %copy-start.1 = (bf16[8,256,128]{2,1,0:T(8,128)(2,1)}, bf16[8,256,128]{2,1,0:T(8,128)(2,1)S(1)}, u32[]{:S(2)}) copy-start(bf16[8,256,128]{2,1,0:T(8,128)(2,1)S(1)} %all-to-all-done) | copy-start | bytes 1572868
  25.3 14.7 %all-to-all-start.1 = ((bf16[8,256,128]{2,1,0:T(8,128)(2,1)}), bf16[8,256,128]{2,1,0:T(8,128)(2,1)S(1)}, u32[]{:S(2)}, u32[]{:S(2)}) async-start(bf16[8,256,128]{2,1,0:T(8,128)(2,1)} %broadcast_in_dim.7), calls=%async_computation.1 | async-start | bytes 1048576 | tf_op jit(solution)/shard_map/all_to_all | solution.py:165
  29.8 10.2 %collective-permute-start = (bf16[2048,128]{1,0:T(8,128)(2,1)S(1)}, bf16[2048,128]{1,0:T(8,128)(2,1)S(1)}, u32[]{:S(2)}, u32[]{:S(2)}) collective-permute-start(bf16[2048,128]{1,0:T(8,128)(2,1)S(1)} %bitcast.25), channel_id=1, source_target_pairs={{0,1},{1,0},{2,3},{3,2},{4,5},{5,4},{6,7},{7,6},{8,9},{9,8},{10,11... | collective-permute-start | bytes 1572872 | tf_op jit(solution)/shard_map/ppermute | solution.py:168
  40.0 0.8 copy-start.2
  40.0 1.0 copy-start.3
  56.4 14.8 %collective-permute-start.1 = (bf16[2048,128]{1,0:T(8,128)(2,1)}, bf16[2048,128]{1,0:T(8,128)(2,1)S(1)}, u32[]{:S(2)}, u32[]{:S(2)}) collective-permute-start(bf16[2048,128]{1,0:T(8,128)(2,1)} %get-tuple-element.7), channel_id=1, source_target_pairs={{0,1},{1,0},{2,3},{3,2},{4,5},{5,4},{6,7},{7,6},{8,9},{9,8},{10,11... | collective-permute-start | bytes 1572872 | tf_op jit(solution)/shard_map/ppermute | solution.py:178
  56.5 25.0 %all-to-all-start.2 = ((bf16[8,256,128]{2,1,0:T(8,128)(2,1)}), bf16[8,256,128]{2,1,0:T(8,128)(2,1)S(1)}, u32[]{:S(2)}, u32[]{:S(2)}) async-start(bf16[8,256,128]{2,1,0:T(8,128)(2,1)} %bitcast.28), calls=%async_computation.2 | async-start | bytes 1048576 | tf_op jit(solution)/shard_map/all_to_all | solution.py:176
  71.2 29.0 %copy-start.5 = (f32[4096]{0:T(1024)S(1)}, f32[4096]{0:T(1024)}, u32[]{:S(2)}) copy-start(f32[4096]{0:T(1024)} %param.7) | copy-start | bytes 49156
  71.2 29.0 %copy-start.6 = (f32[4096]{0:T(1024)S(1)}, f32[4096]{0:T(1024)}, u32[]{:S(2)}) copy-start(f32[4096]{0:T(1024)} %param.8) | copy-start | bytes 49156
  81.5 15.2 %all-to-all-start.3 = ((bf16[8,256,128]{2,1,0:T(8,128)(2,1)}), bf16[8,256,128]{2,1,0:T(8,128)(2,1)S(1)}, u32[]{:S(2)}, u32[]{:S(2)}) async-start(bf16[8,256,128]{2,1,0:T(8,128)(2,1)} %bitcast.6), calls=%async_computation.3 | async-start | bytes 1048576 | tf_op jit(solution)/shard_map/all_to_all | solution.py:176
  114.1 0.9 copy-start.7
